TPU v7x, 512 devices: a whole 4x8x8 slice. The times are simulated.
512 devices in a mesh: row: 64 (over z, y_hi, core), col: 8 (over y_lo, x).
Axes of the slice: x: 4, y: 8 (y_hi: 4, y_lo: 2; y = y_hi * 2 + y_lo), z: 8, core: 2. Of those that a mesh axis runs over, the one named last changes fastest.
Arguments:
- left_projection: bfloat16 [128, 512, 32], P('col', 'row'), may hold values from -6 to 6
- right_projection: bfloat16 [128, 512, 32], P('row', 'col'), may hold values from -6 to 6
- output_weight: bfloat16 [1024, 128], replicated, may hold values from -0.1875 to 0.1875
- pair_update_gradient: bfloat16 [512, 512, 128], P('row', 'col'), may hold values from -6 to 6
- alignment_mask: int32 [128, 512], replicated, may hold values from 0 to 1, as said below
Outputs:
- first_factor_derivative: bfloat16 [128, 512, 32], P('col', 'row')
- grad_right: bfloat16 [128, 512, 32], P('row', 'col')
- grad_wout: float32 [1024, 128], replicated
- grad_bias: float32 [128], replicated
Inputs may be any that keep to these rules, and one draw needn't show every extreme that they name: `alignment_mask`: the last residues of the crop, from 1 to 4 of them, are 0 in every 128 row.
All inputs are finite; a program needn't handle non-finite values.
Results may differ from a plain program's by a relative error of at most 0.0058.
Values may be sent and summed in bfloat16 or wider, within the bound.
No kernel may reach another device: no remote copies, remote signals or barrier semaphores. Data moves between devices by JAX's collectives and lax.ppermute only.
A program may use at most 64 MiB of HBM per device.

v0:
```python
import jax
import jax.numpy as jnp
from jax import lax
from jax.sharding import PartitionSpec as P


def per_device(
    left_projection, right_projection, output_weight, pair_update_gradient, alignment_mask
):
    block_row_span, block_column_span, pair_width = pair_update_gradient.shape
    channel_total = left_projection.shape[2]
    alignment_row_total = alignment_mask.shape[0]
    row_start = lax.axis_index("row") * block_row_span
    column_start = lax.axis_index("col") * block_column_span
    mask_row_view = lax.dynamic_slice_in_dim(alignment_mask, row_start, block_row_span, 1).astype(
        jnp.bfloat16
    )
    mask_column_view = lax.dynamic_slice_in_dim(
        alignment_mask, column_start, block_column_span, 1
    ).astype(jnp.bfloat16)
    counts = jnp.dot(mask_row_view.T, mask_column_view, preferred_element_type=jnp.float32)
    scaled_f = pair_update_gradient.astype(jnp.float32) / jnp.maximum(counts, 1.0)[:, :, None]
    bias_sum = jnp.sum(scaled_f, axis=(0, 1))
    scaled = scaled_f.astype(jnp.bfloat16)
    left_full = lax.all_gather(left_projection, "col", axis=0, tiled=True)
    right_full = lax.all_gather(right_projection, "row", axis=0, tiled=True)
    masked_left_rows = left_full * mask_row_view[:, :, None]
    right_masked = right_full * mask_column_view[:, :, None]
    rows_per_block = 8
    number_of_blocks = block_row_span // rows_per_block
    pair_blocks = scaled.reshape(number_of_blocks, rows_per_block * block_column_span, pair_width)
    left_row_blocks = masked_left_rows.reshape(
        alignment_row_total, number_of_blocks, rows_per_block, channel_total
    ).transpose(1, 0, 2, 3)

    def block_step(totals, pieces):
        weight_sum, right_sum = totals
        pair_flat, left_block = pieces
        grad_outer = jnp.einsum(
            "pk,ok->po", pair_flat, output_weight, preferred_element_type=jnp.float32
        ).astype(jnp.bfloat16)
        grad_outer = grad_outer.reshape(
            rows_per_block, block_column_span, channel_total, channel_total
        )
        outer_tile = jnp.einsum(
            "sic,sjd->ijcd", left_block, right_masked, preferred_element_type=jnp.float32
        ).astype(jnp.bfloat16)
        outer_flat = outer_tile.reshape(
            rows_per_block * block_column_span, channel_total * channel_total
        )
        weight_sum = weight_sum + jnp.einsum(
            "po,pk->ok", outer_flat, pair_flat, preferred_element_type=jnp.float32
        )
        left_grad = jnp.einsum(
            "ijcd,sjd->sic", grad_outer, right_masked, preferred_element_type=jnp.float32
        )
        right_sum = right_sum + jnp.einsum(
            "ijcd,sic->sjd", grad_outer, left_block, preferred_element_type=jnp.float32
        )
        return ((weight_sum, right_sum), left_grad)

    starting_carry = (
        jnp.zeros((channel_total * channel_total, pair_width), jnp.float32),
        jnp.zeros((alignment_row_total, block_column_span, channel_total), jnp.float32),
    )
    totals, first_factor_portions = lax.scan(
        block_step, starting_carry, (pair_blocks, left_row_blocks)
    )
    weight_sum, right_sum = totals
    first_factor_summands = first_factor_portions.transpose(1, 0, 2, 3).reshape(
        alignment_row_total, block_row_span, channel_total
    )
    first_factor_reduced = lax.psum_scatter(
        first_factor_summands, "col", scatter_dimension=0, tiled=True
    )
    left_share = first_factor_reduced.shape[0]
    left_mask = lax.dynamic_slice_in_dim(
        mask_row_view, lax.axis_index("col") * left_share, left_share, 0
    )
    first_factor_derivative = (first_factor_reduced * left_mask[:, :, None]).astype(jnp.bfloat16)
    right_summed = lax.psum_scatter(right_sum, "row", scatter_dimension=0, tiled=True)
    right_share = right_summed.shape[0]
    right_mask = lax.dynamic_slice_in_dim(
        mask_column_view, lax.axis_index("row") * right_share, right_share, 0
    )
    grad_right = (right_summed * right_mask[:, :, None]).astype(jnp.bfloat16)
    grad_wout, grad_bias = lax.psum((weight_sum, bias_sum), ("row", "col"))
    return (first_factor_derivative, grad_right, grad_wout, grad_bias)


def solution(mesh):
    return jax.shard_map(
        per_device,
        mesh=mesh,
        in_specs=(P("col", "row", None), P("row", "col", None), P(), P("row", "col", None), P()),
        out_specs=(P("col", "row", None), P("row", "col", None), P(), P()),
        check_vma=False,
    )
```

profile of v0, /device:TPU:1, one launch (start us, length us, event | category | flops | bytes accessed | tf_op | source)
XLA Modules:
  0.0 444.6 jit_solution(8002552018253836575)
XLA Ops:
  8.0 0.0 copy-start
  8.0 0.0 reduce-scatter.3.cloned.1.call-start
  8.1 1.0 dynamic-slice_convert_fusion
  9.0 0.0 copy-start.1
  9.0 0.1 copy.40
  9.1 0.9 constant_dynamic-slice_fusion.1
  10.1 0.1 copy.60
  10.1 0.0 copy-start.2
  10.1 0.1 convolution_maximum_fusion
  10.3 1.6 fusion.11
  11.9 0.0 copy-done.1
  11.9 0.0 copy-done.2
  11.9 0.0 copy-done
  11.9 0.4 convolution_convert_fusion
  12.3 0.5 copy.43
  12.9 1.1 reshape.28
  14.0 98.9 %all_gather.6 = bf16[128,64,32]{1,2,0:T(8,128)(2,1)} all-gather(bf16[2,64,32]{1,2,0:T(8,128)(2,1)} %param.6), channel_id=1, replica_groups=mesh['row'=64,'col'=8] {'row'}, dimensions={0}, use_global_device_ids=true | all-gather | bytes 532480 | tf_op jit(solution)/shard_map/all_gather | solution.py:26
  112.8 2.8 copy.41
  115.7 4.8 %copy.52 = bf16[8,64,32,32]{2,3,1,0:T(8,128)(2,1)} copy(bf16[8,64,32,32]{1,0,3,2:T(8,128)(2,1)S(1)} %reshape.28) | data formatting | bytes 2097152 | tf_op jit(solution)/shard_map/while/body/eval_jaxpr/reshape | solution.py:42
  120.5 3.7 convolution_bitcast_fusion
  124.2 0.0 reduce-scatter.3.cloned.1.call-update
  124.2 0.0 reduce-scatter.5.cloned.1.call-start
  124.3 0.0 copy-done.5
  124.3 23.7 %all_gather.7 = bf16[128,8,32]{2,1,0:T(8,128)(2,1)S(1)} all-gather(bf16[16,8,32]{2,1,0:T(8,128)(2,1)S(1)} %copy-done.5), channel_id=1, replica_groups=mesh['row'=64,'col'=8] {'col'}, dimensions={0}, use_global_device_ids=true | all-gather | bytes 73728 | tf_op jit(solution)/shard_map/all_gather | solution.py:25
  148.0 0.2 copy.46
  148.2 0.0 copy-done.3
  148.2 2.4 fusion.2
  150.6 4.0 copy.48
  154.7 0.0 reduce-scatter.5.cloned.1.call-update
  154.7 0.2 all-reduce.2.cloned.1.call-start
  154.9 3.2 convert_bitcast_fusion
  158.1 7.8 %copy.49 = bf16[8,64,32,32]{1,0,3,2:T(8,128)(2,1)S(1)} copy(bf16[8,64,32,32]{2,3,0,1:T(8,128)(2,1)} %convert_bitcast_fusion) | data formatting | bytes 2097152 | tf_op jit(solution)/shard_map/while/body/eval_jaxpr/convert_element_type | solution.py:47
  165.9 0.0 copy-start.4
  165.9 0.0 copy-start.6
  166.0 1.3 reshape.29
  167.2 1.2 fusion.20
  168.5 0.0 all-reduce.2.cloned.1.call-update
  168.5 0.7 fusion.19
  169.2 0.0 copy-done.4
  169.2 0.1 dynamic-slice_convert_fusion.1
  169.3 0.0 copy-done.6
  169.3 100.3 %psum.15 = f32[128]{0:T(128)} all-reduce(f32[128]{0:T(128)S(1)} %copy-done.6), channel_id=1, replica_groups=mesh['row'=64,'col'=8] {'row','col'}, use_global_device_ids=true, to_apply=%region_4.5 | all-reduce | flops 128 | bytes 1024 | tf_op jit(solution)/shard_map/psum | solution.py:87
  269.5 0.9 multiply_convert_fusion
  270.5 0.6 copy.50
  271.1 37.8 %reduce-scatter.5.cloned.1.call-done = f32[2,64,32]{1,2,0:T(8,128)} async-done(((f32[128,64,32]{1,2,0:T(8,128)}), f32[2,64,32]{1,2,0:T(8,128)}) %reduce-scatter.5.cloned.1.call-update) | async-done | bytes 16400 | tf_op jit(solution)/shard_map/reduce_scatter | solution.py:81
  308.9 1.4 multiply_convert_fusion.1
  310.3 125.0 %all-reduce.2.cloned.1.call-done = f32[1024,128]{1,0:T(8,128)} async-done(((f32[1024,128]{1,0:T(8,128)}), f32[1024,128]{1,0:T(8,128)}) %all-reduce.2.cloned.1.call-update) | async-done | bytes 524304 | tf_op jit(solution)/shard_map/psum | solution.py:87
  435.2 1.9 copy.66
  (4 shorter events, 0.0 us)
Async XLA Ops:
  8.0 3.9 copy-start
  8.0 261.5 %reduce-scatter.3.cloned.1.call-start = ((), (), s32[]{:S(2)}) async-start(), calls=%async_computation.2 | async-start | bytes 589824 | tf_op jit(solution)/shard_map/reduce_scatter | solution.py:73
  9.0 2.8 copy-start.1
  10.1 1.7 copy-start.2
  120.5 3.8 copy-start.5
  120.5 27.8 %copy-start.3 = (bf16[128,8]{0,1:T(8,128)(2,1)S(1)}, bf16[128,8]{0,1:T(8,128)(2,1)}, u32[]{:S(2)}) copy-start(bf16[128,8]{0,1:T(8,128)(2,1)} %copy-done.2) | copy-start | bytes 6148
  124.2 184.7 %reduce-scatter.5.cloned.1.call-start = ((), (), s32[]{:S(2)}) async-start(), calls=%async_computation.3 | async-start | bytes 2129920 | tf_op jit(solution)/shard_map/reduce_scatter | solution.py:81
  154.7 280.6 %all-reduce.2.cloned.1.call-start = ((), (), s32[]{:S(2)}) async-start(), calls=%async_computation.4 | async-start | bytes 1048576 | tf_op jit(solution)/shard_map/psum | solution.py:87
  165.9 3.2 copy-start.4
  165.9 3.3 copy-start.6
Sparse Core Ops, SparseCore 0:
  124.3 28.9 reduce-scatter.2
  158.7 150.1 reduce-scatter.4
Sparse Core Ops, SparseCore 1:
  168.6 266.6 all-reduce.1
where the time goes:
time: 445 us
  blocking collectives  223 us (50%)
  waiting for transfers between devices  163 us (37%)
  local copies, waits for them, and re-layouts  26.1 us (6%)
  between operations  15.6 us (4%)
  matrix products  11.2 us (3%)
  other arithmetic  5.59 us (1%)
    psum x1, waiting for transfers between devices, per_device(): grad_wout, grad_bias = lax.psum((weight_sum, bias_sum), ('row', 'col'))  125 us
    psum x1, blocking collectives, per_device(): grad_wout, grad_bias = lax.psum((weight_sum, bias_sum), ('row', 'col'))  100 us
    all_gather x1, blocking collectives, per_device(): right_full = lax.all_gather(right_projection, 'row', axis=0, tiled=True)  98.9 us
    reduce_scatter x1, waiting for transfers between devices, per_device(): lax.psum_scatter(right_sum, 'row', scatter_dimension=0, tiled=True)  37.8 us
    all_gather x1, blocking collectives, per_device(): left_full = lax.all_gather(left_projection, 'col', axis=0, tiled=True)  23.7 us
  transfers between devices with their start and end apart: 3, of which 2 were waited for; matrix products, arithmetic and copies ran while one was open for 5% of the time, Pallas kernels for 0%

commit v1 on v0

--- a/solution.py
+++ b/solution.py
@@ -22,7 +22,9 @@
     scaled_f = pair_update_gradient.astype(jnp.float32) / jnp.maximum(counts, 1.0)[:, :, None]
     bias_sum = jnp.sum(scaled_f, axis=(0, 1))
     scaled = scaled_f.astype(jnp.bfloat16)
-    left_full = lax.all_gather(left_projection, "col", axis=0, tiled=True)
+    left_full = jnp.concatenate(
+        lax.all_to_all(jnp.stack([left_projection] * lax.axis_size("col")), "col", 0, 0), axis=0
+    )
     right_full = lax.all_gather(right_projection, "row", axis=0, tiled=True)
     masked_left_rows = left_full * mask_row_view[:, :, None]
     right_masked = right_full * mask_column_view[:, :, None]

time: 445 us -> 527 us (1.18)
  waiting for transfers between devices: 163 us -> 260 us
  blocking collectives: 223 us -> 194 us
  starting transfers between devices: 0.3 us -> 5.98 us
    psum x1, waiting for transfers between devices: 125 us -> 197 us  [per_device(): grad_wout, grad_bias = lax.psum((weight_sum, bias_sum), ('row', 'col'))]
    reduce_scatter x1, waiting for transfers between devices: 37.8 us -> 63.6 us  [per_device(): lax.psum_scatter(right_sum, 'row', scatter_dimension=0, tiled=True)]
    all_gather x1 -> x0, blocking collectives: 23.7 us -> none  [per_device(): left_full = lax.all_gather(left_projection, 'col', axis=0, tiled=True)]
    all_to_all x0 -> x1, starting transfers between devices: none -> 5.86 us  [per_device(): lax.all_to_all(jnp.stack([left_projection] * lax.axis_size('col')), 'col'...]
  transfers between devices with their start and end apart: 3 -> 4, of which waited for: 2 -> 2; matrix products, arithmetic and copies ran while one was open for 5% -> 9% of each run, Pallas kernels for 0% -> 0%
where the time goes in v1:
time: 527 us; the launch traced here: 526 us
  waiting for transfers between devices  260 us (49%)
  blocking collectives  194 us (37%)
  local copies, waits for them, and re-layouts  31.3 us (6%)
  between operations  15.7 us (3%)
  matrix products  11.1 us (2%)
  other arithmetic  7.7 us (1%)
  starting transfers between devices  5.98 us (1%)
    psum x1, waiting for transfers between devices, per_device(): grad_wout, grad_bias = lax.psum((weight_sum, bias_sum), ('row', 'col'))  197 us
    psum x1, blocking collectives, per_device(): grad_wout, grad_bias = lax.psum((weight_sum, bias_sum), ('row', 'col'))  96.9 us
    all_gather x1, blocking collectives, per_device(): right_full = lax.all_gather(right_projection, 'row', axis=0, tiled=True)  96.9 us
    reduce_scatter x1, waiting for transfers between devices, per_device(): lax.psum_scatter(right_sum, 'row', scatter_dimension=0, tiled=True)  63.6 us
  transfers between devices with their start and end apart: 4, of which 2 were waited for; matrix products, arithmetic and copies ran while one was open for 9% of the time, Pallas kernels for 0%

profile of v1, /device:TPU:1, one launch (start us, length us, event | category | flops | bytes accessed | tf_op | source)
XLA Modules:
  0.0 526.0 jit_solution(12431251294752907039)
XLA Ops:
  8.0 0.0 copy-start
  8.0 0.8 stack.2
  8.8 0.9 reshape.42
  9.7 5.9 %all-to-all-start = ((bf16[8,2,2048]{2,1,0:T(2,128)(2,1)}), bf16[8,2,2048]{2,1,0:T(2,128)(2,1)S(1)}, u32[]{:S(2)}, u32[]{:S(2)}) async-start(bf16[8,2,2048]{2,1,0:T(2,128)(2,1)} %reshape.42), calls=%async_computation.1 | async-start | bytes 131072 | tf_op jit(solution)/shard_map/all_to_all | solution.py:26
  15.6 0.0 reduce-scatter.3.cloned.1.call-start
  15.7 0.9 dynamic-slice_convert_fusion
  16.6 0.0 copy-start.1
  16.6 0.1 copy.40
  16.7 0.9 constant_dynamic-slice_fusion.1
  17.6 0.1 copy.62
  17.7 0.1 convolution_maximum_fusion
  17.8 1.6 fusion.11
  19.4 0.0 copy-done.1
  19.4 0.0 copy-done
  19.4 0.4 convolution_convert_fusion
  19.9 1.3 copy.43
  21.2 2.8 reshape.33
  24.0 96.9 %all_gather.3 = bf16[128,64,32]{1,2,0:T(8,128)(2,1)} all-gather(bf16[2,64,32]{1,2,0:T(8,128)(2,1)S(1)} %copy-done.4), channel_id=1, replica_groups=mesh['row'=64,'col'=8] {'row'}, dimensions={0}, use_global_device_ids=true | all-gather | bytes 532480 | tf_op jit(solution)/shard_map/all_gather | solution.py:28
  120.9 2.8 copy.41
  123.7 4.8 copy.54
  128.5 3.7 convolution_bitcast_fusion
  132.2 0.0 reduce-scatter.3.cloned.1.call-update
  132.3 0.0 reduce-scatter.5.cloned.1.call-start
  132.3 0.7 copy.46
  133.1 0.0 all-to-all-done
  133.1 0.2 reshape.43
  133.2 1.0 bitcast_multiply_fusion
  134.2 0.2 copy.47
  134.4 2.4 fusion.2
  136.8 4.1 copy.49
  140.9 0.0 reduce-scatter.5.cloned.1.call-update
  140.9 0.0 all-reduce.2.cloned.1.call-start
  141.0 96.9 %psum.15 = f32[128]{0:T(128)} all-reduce(f32[128]{0:T(128)S(1)} %copy-done.7), channel_id=1, replica_groups=mesh['row'=64,'col'=8] {'row','col'}, use_global_device_ids=true, to_apply=%region_4.5 | all-reduce | flops 128 | bytes 1024 | tf_op jit(solution)/shard_map/psum | solution.py:89
  237.9 1.3 fusion.15
  239.1 0.7 dynamic-slice_convert_fusion.1
  239.8 3.2 convert_bitcast_fusion
  243.0 7.8 %copy.51 = bf16[8,64,32,32]{1,0,3,2:T(8,128)(2,1)S(1)} copy(bf16[8,64,32,32]{2,3,0,1:T(8,128)(2,1)} %convert_bitcast_fusion) | data formatting | bytes 2097152 | tf_op jit(solution)/shard_map/while/body/eval_jaxpr/convert_element_type | solution.py:49
  250.8 0.0 copy-start.5
  250.8 1.3 reshape.35
  252.1 1.2 fusion.16
  253.3 0.0 all-reduce.2.cloned.1.call-update
  253.3 0.0 reduce-scatter.3.cloned.1.call-done
  253.4 0.9 multiply_convert_fusion
  254.3 0.6 copy.52
  254.9 63.6 %reduce-scatter.5.cloned.1.call-done = f32[2,64,32]{1,2,0:T(8,128)} async-done(((f32[128,64,32]{1,2,0:T(8,128)}), f32[2,64,32]{1,2,0:T(8,128)}) %reduce-scatter.5.cloned.1.call-update) | async-done | bytes 16400 | tf_op jit(solution)/shard_map/reduce_scatter | solution.py:83
  318.5 1.4 multiply_convert_fusion.1
  319.9 196.8 %all-reduce.2.cloned.1.call-done = f32[1024,128]{1,0:T(8,128)} async-done(((f32[1024,128]{1,0:T(8,128)}), f32[1024,128]{1,0:T(8,128)}) %all-reduce.2.cloned.1.call-update) | async-done | bytes 524304 | tf_op jit(solution)/shard_map/psum | solution.py:89
  516.7 1.9 copy.68
  (12 shorter events, 0.0 us)
Async XLA Ops:
  8.0 11.4 %copy-start = (bf16[1024,128]{1,0:T(8,128)(2,1)S(1)}, bf16[1024,128]{1,0:T(8,128)(2,1)}, u32[]{:S(2)}) copy-start(bf16[1024,128]{1,0:T(8,128)(2,1)} %param.7) | copy-start | bytes 786436
  9.7 123.3 %all-to-all-start = ((bf16[8,2,2048]{2,1,0:T(2,128)(2,1)}), bf16[8,2,2048]{2,1,0:T(2,128)(2,1)S(1)}, u32[]{:S(2)}, u32[]{:S(2)}) async-start(bf16[8,2,2048]{2,1,0:T(2,128)(2,1)} %reshape.42), calls=%async_computation.1 | async-start | bytes 131072 | tf_op jit(solution)/shard_map/all_to_all | solution.py:26
  15.6 237.8 %reduce-scatter.3.cloned.1.call-start = ((), (), s32[]{:S(2)}) async-start(), calls=%async_computation.3 | async-start | bytes 589824 | tf_op jit(solution)/shard_map/reduce_scatter | solution.py:75
  16.6 2.8 copy-start.1
  17.7 114.6 %copy-start.2 = (bf16[128,8]{0,1:T(8,128)(2,1)}, bf16[128,8]{0,1:T(8,128)(2,1)S(1)}, u32[]{:S(2)}) copy-start(bf16[128,8]{0,1:T(8,128)(2,1)S(1)} %convert_element_type.39) | copy-start | bytes 6148
  21.2 2.8 copy-start.4
  132.3 186.2 %reduce-scatter.5.cloned.1.call-start = ((), (), s32[]{:S(2)}) async-start(), calls=%async_computation.4 | async-start | bytes 2129920 | tf_op jit(solution)/shard_map/reduce_scatter | solution.py:83
  136.8 4.1 copy-start.7
  136.8 102.3 %copy-start.3 = (bf16[128,8]{0,1:T(8,128)(2,1)S(1)}, bf16[128,8]{0,1:T(8,128)(2,1)}, u32[]{:S(2)}) copy-start(bf16[128,8]{0,1:T(8,128)(2,1)} %copy-done.2) | copy-start | bytes 6148
  140.9 375.8 %all-reduce.2.cloned.1.call-start = ((), (), s32[]{:S(2)}) async-start(), calls=%async_computation.5 | async-start | bytes 1048576 | tf_op jit(solution)/shard_map/psum | solution.py:89
  250.8 2.6 copy-start.5
  250.8 67.7 %copy-start.6 = (f32[2,64]{1,0:T(2,128)S(1)}, f32[2,64]{1,0:T(2,128)}, u32[]{:S(2)}) copy-start(f32[2,64]{1,0:T(2,128)} %fusion.15) | copy-start | bytes 1540
Sparse Core Ops, SparseCore 0:
  132.4 30.2 reduce-scatter.2
  168.0 150.4 reduce-scatter.4
Sparse Core Ops, SparseCore 1:
  253.4 263.2 all-reduce.1

commit v2 on v0

--- a/solution.py
+++ b/solution.py
@@ -84,7 +84,7 @@
         mask_column_view, lax.axis_index("row") * right_share, right_share, 0
     )
     grad_right = (right_summed * right_mask[:, :, None]).astype(jnp.bfloat16)
-    grad_wout, grad_bias = lax.psum((weight_sum, bias_sum), ("row", "col"))
+    grad_wout, grad_bias = lax.psum(lax.psum((weight_sum, bias_sum), "row"), "col")
     return (first_factor_derivative, grad_right, grad_wout, grad_bias)
 
 

time: 445 us -> 785 us (1.76)
  waiting for transfers between devices: 163 us -> 444 us
  blocking collectives: 223 us -> 277 us
    psum x1 -> x2, waiting for transfers between devices: 125 us -> 444 us  [the longest x1 370 us: per_device(): lax.psum((weight_sum, bias_sum), 'row')]
    psum x1 -> x2, blocking collectives: 100 us -> 155 us  [the longest x1 138 us: per_device(): lax.psum((weight_sum, bias_sum), 'row')]
    reduce_scatter x1, waiting for transfers between devices: 37.8 us -> 0.01 us  [per_device(): lax.psum_scatter(right_sum, 'row', scatter_dimension=0, tiled=True)]
  transfers between devices with their start and end apart: 3 -> 4, of which waited for: 2 -> 2; matrix products, arithmetic and copies ran while one was open for 5% -> 3% of each run, Pallas kernels for 0% -> 0%
where the time goes in v2:
time: 785 us; the launch traced here: 781 us
  waiting for transfers between devices  444 us (57%)
  blocking collectives  277 us (35%)
  local copies, waits for them, and re-layouts  28.2 us (4%)
  between operations  15.8 us (2%)
  matrix products  12.4 us (2%)
    psum x1, waiting for transfers between devices, per_device(): lax.psum((weight_sum, bias_sum), 'row')  370 us
    psum x1, blocking collectives, per_device(): lax.psum((weight_sum, bias_sum), 'row')  138 us
    all_gather x1, blocking collectives, per_device(): right_full = lax.all_gather(right_projection, 'row', axis=0, tiled=True)  98.5 us
    psum x1, waiting for transfers between devices, per_device(): lax.psum(lax.psum((weight_sum, bias_sum), 'row'), 'col')  73.9 us
    all_gather x1, blocking collectives, per_device(): left_full = lax.all_gather(left_projection, 'col', axis=0, tiled=True)  23.5 us
    psum x1, blocking collectives, per_device(): lax.psum(lax.psum((weight_sum, bias_sum), 'row'), 'col')  16.2 us
  transfers between devices with their start and end apart: 4, of which 2 were waited for; matrix products, arithmetic and copies ran while one was open for 3% of the time, Pallas kernels for 0%

profile of v2, /device:TPU:1, one launch (start us, length us, event | category | flops | bytes accessed | tf_op | source)
XLA Modules:
  0.0 780.6 jit_solution(8008193621182842589)
XLA Ops:
  8.0 0.0 copy-start
  8.0 0.0 all-reduce.3.cloned.1.call-start
  8.1 1.0 dynamic-slice_convert_fusion
  9.0 0.1 copy.40
  9.1 0.9 constant_dynamic-slice_fusion.1
  10.1 0.1 copy.60
  10.1 0.1 convolution_maximum_fusion
  10.3 23.5 %all_gather.7 = bf16[128,8,32]{2,1,0:T(8,128)(2,1)S(1)} all-gather(bf16[16,8,32]{2,1,0:T(8,128)(2,1)} %param.5), channel_id=1, replica_groups=mesh['row'=64,'col'=8] {'col'}, dimensions={0}, use_global_device_ids=true | all-gather | bytes 73728 | tf_op jit(solution)/shard_map/all_gather | solution.py:25
  33.8 0.2 copy.46
  34.0 98.5 %all_gather.6 = bf16[128,64,32]{1,2,0:T(8,128)(2,1)S(1)} all-gather(bf16[2,64,32]{1,2,0:T(8,128)(2,1)} %param.6), channel_id=1, replica_groups=mesh['row'=64,'col'=8] {'row'}, dimensions={0}, use_global_device_ids=true | all-gather | bytes 532480 | tf_op jit(solution)/shard_map/all_gather | solution.py:26
  132.4 1.5 copy.41
  134.0 3.2 convert_bitcast_fusion
  137.2 7.8 copy.49
  145.0 0.0 copy-start.1
  145.0 2.1 reshape.29
  147.1 0.0 copy-done.1
  147.1 0.2 fusion.11
  147.2 2.5 fusion.20
  149.7 0.0 all-reduce.3.cloned.1.call-update
  149.8 0.0 reduce-scatter.3.cloned.1.call-start
  149.8 0.0 copy-done
  149.8 0.4 convolution_convert_fusion
  150.3 1.3 copy.43
  151.6 2.8 reshape.28
  154.4 4.8 copy.52
  159.2 3.7 convolution_bitcast_fusion
  162.9 0.0 reduce-scatter.3.cloned.1.call-update
  162.9 0.2 reduce-scatter.5.cloned.1.call-start
  163.2 2.4 fusion.2
  165.6 4.1 copy.48
  169.7 0.0 reduce-scatter.5.cloned.1.call-update
  169.7 0.0 all-reduce.5.cloned.1.call-start
  169.7 138.5 %psum.30 = f32[128]{0:T(128)S(1)} all-reduce(f32[128]{0:T(128)S(1)} %get-tuple-element.44), channel_id=1, replica_groups=mesh['row'=64,'col'=8] {'row'}, use_global_device_ids=true, to_apply=%region_5.6 | all-reduce | flops 128 | bytes 1024 | tf_op jit(solution)/shard_map/psum | solution.py:87
  308.2 16.2 %psum.31 = f32[128]{0:T(128)} all-reduce(f32[128]{0:T(128)S(1)} %psum.30), channel_id=1, replica_groups=mesh['row'=64,'col'=8] {'col'}, use_global_device_ids=true, to_apply=%region_6.7 | all-reduce | flops 128 | bytes 1024 | tf_op jit(solution)/shard_map/psum | solution.py:87
  324.4 0.1 dynamic-slice_convert_fusion.1
  324.5 369.7 %all-reduce.3.cloned.1.call-done = f32[1024,128]{1,0:T(8,128)} async-done(((f32[1024,128]{1,0:T(8,128)}), f32[1024,128]{1,0:T(8,128)}) %all-reduce.3.cloned.1.call-update) | async-done | bytes 524304 | tf_op jit(solution)/shard_map/psum | solution.py:87
  694.3 0.0 all-reduce.5.cloned.1.call-update
  694.3 0.0 reduce-scatter.3.cloned.1.call-done
  694.3 0.9 multiply_convert_fusion
  695.3 0.6 copy.50
  695.9 0.0 reduce-scatter.5.cloned.1.call-done
  695.9 1.4 multiply_convert_fusion.1
  697.3 73.9 %all-reduce.5.cloned.1.call-done = f32[1024,128]{1,0:T(8,128)} async-done(((f32[1024,128]{1,0:T(8,128)}), f32[1024,128]{1,0:T(8,128)}) %all-reduce.5.cloned.1.call-update) | async-done | bytes 524304 | tf_op jit(solution)/shard_map/psum | solution.py:87
  771.1 1.9 copy.67
  (2 shorter events, 0.0 us)
Async XLA Ops:
  8.0 141.8 %copy-start = (bf16[1024,128]{1,0:T(8,128)(2,1)S(1)}, bf16[1024,128]{1,0:T(8,128)(2,1)}, u32[]{:S(2)}) copy-start(bf16[1024,128]{1,0:T(8,128)(2,1)} %param.7) | copy-start | bytes 786436
  8.0 686.2 %all-reduce.3.cloned.1.call-start = ((), (), s32[]{:S(2)}) async-start(), calls=%async_computation.4 | async-start | bytes 1048576 | tf_op jit(solution)/shard_map/psum | solution.py:87
  145.0 2.1 copy-start.1
  149.8 544.6 %reduce-scatter.3.cloned.1.call-start = ((), (), s32[]{:S(2)}) async-start(), calls=%async_computation.2 | async-start | bytes 589824 | tf_op jit(solution)/shard_map/reduce_scatter | solution.py:73
  162.9 533.0 %reduce-scatter.5.cloned.1.call-start = ((), (), s32[]{:S(2)}) async-start(), calls=%async_computation.3 | async-start | bytes 2129920 | tf_op jit(solution)/shard_map/reduce_scatter | solution.py:81
  169.7 601.4 %all-reduce.5.cloned.1.call-start = ((), (), s32[]{:S(2)}) async-start(), calls=%async_computation.5 | async-start | bytes 1048576 | tf_op jit(solution)/shard_map/psum | solution.py:87
Sparse Core Ops, SparseCore 0:
  149.9 544.3 all-reduce.2
Sparse Core Ops, SparseCore 1:
  163.0 29.0 reduce-scatter.2
  197.2 150.5 reduce-scatter.4
  694.4 76.7 all-reduce.4
